TPU v7x, 32 devices: a whole 2x2x4 slice. The times are simulated.
32 devices in a mesh: batch: 4 (over z), mp: 8 (over y, x, core).
Axes of the slice: x: 2, y: 2, z: 4, core: 2. Of those that a mesh axis runs over, the one named last changes fastest.
Arguments:
- hidden_in: bfloat16 [128, 16384], P('batch'), may hold values from -36 to 36
- queries: bfloat16 [128, 16384], P('batch', 'mp'), may hold values from -128 to 128
- key_cache: bfloat16 [128, 1024], P('batch'), may hold values from -4.5 to 4.5
- value_cache: bfloat16 [128, 1024], P('batch'), may hold values from -4 to 4
- question: int32 [32], P('batch'), may hold values from 0 to 3
- prefix_len: int32 [4], replicated, may hold values from 6 to 24, as said below
- norm_gain: float32 [16384], replicated, may hold values from 0.1 to 1.9
- gate_weight: bfloat16 [16384, 26624], P('batch', 'mp'), may hold values from -0.046875 to 0.046875
- up_weight: bfloat16 [16384, 26624], P('batch', 'mp'), may hold values from -0.046875 to 0.046875
- down_weight: bfloat16 [26624, 16384], P('mp', 'batch'), may hold values from -0.0390625 to 0.0390625
Outputs:
- layer_out: bfloat16 [128, 16384], P('mp', 'batch')
Inputs may be any that keep to these rules, and one draw needn't show every extreme that they name: `prefix_len`: some question has all 24 prefix tokens live, and another question has the fewest allowed.
All inputs are finite; a program needn't handle non-finite values.
Results may differ from a plain program's by a relative error of at most 0.0055.
Values may be sent and summed in bfloat16 or wider, within the bound.
A program may use at most 128 MiB of HBM per device.

v0:
```python
import jax
import jax.numpy as jnp
from jax import lax
from jax.sharding import PartitionSpec as P

HEADS = 128
KV_HEADS = 8
HEAD_DIM = 128
PREFIX = 24
ROWS_DEV = 32


def attend(batch_index, first_group, query_block, key_cache, value_cache, question, prefix_len):
    group_size = HEADS // KV_HEADS
    local_heads = query_block.shape[1] // HEAD_DIM
    per_group = min(local_heads, group_size)
    group_count = local_heads // per_group
    total_rows = key_cache.shape[0]
    local_rows = jnp.arange(ROWS_DEV, dtype=jnp.int32)
    owner_rows = jnp.concatenate([jnp.zeros((PREFIX,), jnp.int32) + batch_index, question])
    owner_length = prefix_len[owner_rows]
    key_limit = jnp.where(
        local_rows < PREFIX, jnp.minimum(local_rows + 1, owner_length), owner_length
    )
    key_index = jnp.arange(total_rows, dtype=jnp.int32)
    key_batch = key_index // ROWS_DEV
    key_local = key_index % ROWS_DEV
    own_index = batch_index * ROWS_DEV + local_rows
    allowed = (key_batch[None, :] == owner_rows[:, None]) & (
        key_local[None, :] < key_limit[:, None]
    ) | (key_index[None, :] == own_index[:, None]) & (local_rows[:, None] >= PREFIX)
    key_heads = lax.dynamic_slice_in_dim(
        key_cache, first_group * HEAD_DIM, group_count * HEAD_DIM, 1
    ).reshape(total_rows, group_count, HEAD_DIM)
    value_heads = lax.dynamic_slice_in_dim(
        value_cache, first_group * HEAD_DIM, group_count * HEAD_DIM, 1
    ).reshape(total_rows, group_count, HEAD_DIM)
    query_heads = query_block.reshape(ROWS_DEV, group_count, per_group, HEAD_DIM)
    scores = jnp.einsum(
        "rgpd,kgd->gprk", query_heads, key_heads, preferred_element_type=jnp.float32
    ) / jnp.sqrt(jnp.float32(HEAD_DIM))
    scores = jnp.where(allowed[None, None], scores, jnp.float32(-1e30))
    row_peak = jnp.max(scores, axis=-1, keepdims=True)
    exponent = jnp.exp(scores - row_peak)
    attention = (exponent / jnp.sum(exponent, axis=-1, keepdims=True)).astype(jnp.bfloat16)
    context = jnp.einsum(
        "gprk,kgd->rgpd", attention, value_heads, preferred_element_type=jnp.float32
    )
    return context.reshape(ROWS_DEV, local_heads * HEAD_DIM).astype(jnp.bfloat16)


def body(
    hidden_in,
    queries,
    key_cache,
    value_cache,
    question,
    prefix_len,
    norm_gain,
    gate_weight,
    up_weight,
    down_weight,
):
    batch_index = lax.axis_index("batch")
    column_index = lax.axis_index("mp")
    all_keys, all_values = (
        lax.all_gather(key_cache, "batch", axis=0, tiled=True),
        lax.all_gather(value_cache, "batch", axis=0, tiled=True),
    )
    local_heads = queries.shape[1] // HEAD_DIM
    first_group = column_index * local_heads // (HEADS // KV_HEADS)
    context = attend(batch_index, first_group, queries, all_keys, all_values, question, prefix_len)
    full_context = lax.all_gather(context, "mp", axis=1, tiled=True)
    residual = (hidden_in.astype(jnp.float32) + full_context.astype(jnp.float32)).astype(
        jnp.bfloat16
    )
    widened = residual.astype(jnp.float32)
    mean_square = jnp.mean(widened * widened, axis=-1, keepdims=True)
    normed = (widened * lax.rsqrt(mean_square + 1e-05) * norm_gain).astype(jnp.bfloat16)
    normed_all, residual_all = (
        lax.all_to_all(normed, "batch", split_axis=1, concat_axis=0, tiled=True),
        lax.all_to_all(residual, "batch", split_axis=1, concat_axis=0, tiled=True),
    )
    total_rows = normed_all.shape[0]
    hidden_width = gate_weight.shape[1]
    gate_up = jnp.concatenate([gate_weight, up_weight], axis=1)
    out_rows = total_rows // lax.axis_size("mp")
    partial_sums = jnp.dot(normed_all, gate_up, preferred_element_type=jnp.float32)
    summed = lax.psum(partial_sums, "batch")
    hidden = (jax.nn.silu(summed[:, :hidden_width]) * summed[:, hidden_width:]).astype(jnp.bfloat16)
    branch_out = lax.psum_scatter(
        jnp.dot(hidden, down_weight, preferred_element_type=jnp.float32),
        "mp",
        scatter_dimension=0,
        tiled=True,
    )
    own_rows = lax.dynamic_slice_in_dim(residual_all, column_index * out_rows, out_rows, 0)
    return (own_rows.astype(jnp.float32) + branch_out).astype(jnp.bfloat16)


def solution(mesh):
    return jax.shard_map(
        body,
        mesh=mesh,
        in_specs=(
            P("batch", None),
            P("batch", "mp"),
            P("batch", None),
            P("batch", None),
            P("batch"),
            P(),
            P(),
            P("batch", "mp"),
            P("batch", "mp"),
            P("mp", "batch"),
        ),
        out_specs=P("mp", "batch"),
        check_vma=False,
    )
```

profile of v0, /device:TPU:0, one launch (start us, length us, event | category | flops | bytes accessed | tf_op | source)
XLA Modules:
  0.0 313.0 jit_solution(9708323313243962327)
XLA Ops:
  6.6 0.8 concatenate.6
  7.4 1.5 fusion.28
  8.9 15.8 %all_gather.10 = bf16[128,1024]{1,0:T(8,128)(2,1)S(1)} all-gather(bf16[32,1024]{1,0:T(8,128)(2,1)} %param.12), channel_id=1, replica_groups=mesh['batch'=4,'mp'=8] {'batch'}, dimensions={0}, use_global_device_ids=true | all-gather | bytes 327680 | tf_op jit(solution)/shard_map/all_gather | solution.py:67
  24.7 14.8 %all_gather.9 = bf16[128,1024]{1,0:T(8,128)(2,1)S(1)} all-gather(bf16[32,1024]{1,0:T(8,128)(2,1)} %param.13), channel_id=1, replica_groups=mesh['batch'=4,'mp'=8] {'batch'}, dimensions={0}, use_global_device_ids=true | all-gather | bytes 327680 | tf_op jit(solution)/shard_map/all_gather | solution.py:68
  39.6 3.2 %compare_select_fusion.4 = (s32[32]{0:T(128)S(1)}, s32[32]{0:T(128)S(1)}) fusion(s32[]{:T(128)} %bitcast.1, s32[]{:T(128)} %bitcast.2, s32[]{:T(128)} %bitcast.3, s32[]{:T(128)} %bitcast.4, s32[]{:T(128)S(6)} %mul.39, s32[8]{0:T(128)} %param.14, s32[]{:T(128)S(6)} %axis_index.25), kind=kLoop, calls=%fused_computation.40 | loop fusion | flops 448 | bytes 312 | tf_op jit(solution)/shard_map/jit(_where)/select_n | solution.py:22
  42.8 0.1 fusion.23
  42.9 0.3 fusion.29
  43.2 0.3 fusion.14
  43.4 0.3 fusion.10
  43.8 0.1 copy.14
  43.8 0.7 copy.32
  44.6 24.6 %all-gather.2.cloned.1.call-done = bf16[32,16384]{1,0:T(8,128)(2,1)} async-done(((bf16[32,2048]{1,0:T(8,128)(2,1)}), bf16[32,16384]{1,0:T(8,128)(2,1)}) %all-gather.2.cloned.1.call-update) | async-done | bytes 1048592 | tf_op jit(solution)/shard_map/all_gather | solution.py:73
  69.1 1.7 fusion.4
  70.9 0.3 fusion.6
  71.2 0.1 copy.30
  71.3 30.6 %all_to_all.38 = bf16[32,4,4096]{2,0,1:T(8,128)(2,1)S(1)} all-to-all(bf16[32,4,4096]{2,0,1:T(8,128)(2,1)S(1)} %bitcast.58), channel_id=1, replica_groups=mesh['batch'=4,'mp'=8] {'batch'}, dimensions={1} | all-to-all | bytes 2097152 | tf_op jit(solution)/shard_map/all_to_all | solution.py:81
  101.8 19.7 %fusion = f32[128,6656]{1,0:T(8,128)} fusion(bf16[128,4096]{1,0:T(8,128)(2,1)S(1)} %bitcast.60, bf16[4096,3328]{1,0:T(8,128)(2,1)} %param.18, bf16[4096,3328]{1,0:T(8,128)(2,1)} %param.17), kind=kOutput, calls=%fused_computation | convolution fusion | flops 7088373760 | bytes 58982400 | tf_op jit(solution)/shard_map/dot_general | solution.py:88
  121.6 127.8 %all-reduce.3.cloned.1.call-done = f32[128,6656]{1,0:T(8,128)} async-done(((f32[128,6656]{1,0:T(8,128)}), f32[128,6656]{1,0:T(8,128)}) %all-reduce.3.cloned.1.call-update) | async-done | bytes 3407888 | tf_op jit(solution)/shard_map/psum | solution.py:89
  249.4 15.0 %fusion.11 = f32[128,4096]{1,0:T(8,128)} fusion(bf16[3328,4096]{1,0:T(8,128)(2,1)} %param.19, f32[128,6656]{1,0:T(8,128)} %all-reduce.3.cloned.1.call-done), kind=kOutput, calls=%fused_computation.19 | convolution fusion | flops 3492216832 | bytes 32768000 | tf_op jit(solution)/shard_map/dot_general | solution.py:92
  264.4 1.0 copy.31
  265.5 3.5 %all-to-all-start = ((bf16[32,4,4096]{2,0,1:T(8,128)(2,1)}), bf16[32,4,4096]{2,0,1:T(8,128)(2,1)S(1)}, u32[]{:S(2)}, u32[]{:S(2)}) async-start(bf16[32,4,4096]{2,0,1:T(8,128)(2,1)} %bitcast.54), calls=%async_computation | async-start | bytes 2097152 | tf_op jit(solution)/shard_map/all_to_all | solution.py:82
  269.0 25.9 %all-to-all-done = bf16[32,4,4096]{2,0,1:T(8,128)(2,1)S(1)} async-done(((bf16[32,4,4096]{2,0,1:T(8,128)(2,1)}), bf16[32,4,4096]{2,0,1:T(8,128)(2,1)S(1)}, u32[]{:S(2)}, u32[]{:S(2)}) %all-to-all-start) | async-done | bytes 1048608 | tf_op jit(solution)/shard_map/all_to_all | solution.py:82
  294.9 9.9 %reduce-scatter.2.cloned.1.call-done = f32[16,4096]{1,0:T(8,128)} async-done(((f32[128,4096]{1,0:T(8,128)}), f32[16,4096]{1,0:T(8,128)}) %reduce-scatter.2.cloned.1.call-update) | async-done | bytes 262160 | tf_op jit(solution)/shard_map/reduce_scatter | solution.py:91
  304.8 1.6 add_convert_fusion.1
  (17 shorter events, 0.2 us)
Async XLA Ops:
  6.5 36.3 %copy-start = (bf16[32,2048]{1,0:T(8,128)(2,1)S(1)}, bf16[32,2048]{1,0:T(8,128)(2,1)}, u32[]{:S(2)}) copy-start(bf16[32,2048]{1,0:T(8,128)(2,1)} %param.11) | copy-start | bytes 393220
  6.5 62.6 %copy-start.2 = (bf16[32,16384]{1,0:T(8,128)(2,1)S(1)}, bf16[32,16384]{1,0:T(8,128)(2,1)}, u32[]{:S(2)}) copy-start(bf16[32,16384]{1,0:T(8,128)(2,1)} %param.10) | copy-start | bytes 3145732
  6.5 64.3 %copy-start.3 = (f32[16384]{0:T(1024)S(1)}, f32[16384]{0:T(1024)}, u32[]{:S(2)}) copy-start(f32[16384]{0:T(1024)} %param.16) | copy-start | bytes 196612
  6.5 62.6 %all-gather.2.cloned.1.call-start = ((), (), s32[]{:S(2)}) async-start(), calls=%async_computation.3 | async-start | bytes 1179648 | tf_op jit(solution)/shard_map/all_gather | solution.py:73
  44.5 204.8 %all-reduce.3.cloned.1.call-start = ((), (), s32[]{:S(2)}) async-start(), calls=%async_computation.4 | async-start | bytes 6815744 | tf_op jit(solution)/shard_map/psum | solution.py:89
  121.5 183.3 %reduce-scatter.2.cloned.1.call-start = ((), (), s32[]{:S(2)}) async-start(), calls=%async_computation.5 | async-start | bytes 2359296 | tf_op jit(solution)/shard_map/reduce_scatter | solution.py:91
  264.4 42.0 %copy-start.1 = (bf16[32,2048]{1,0:T(8,128)(2,1)S(1)}, bf16[32,2048]{1,0:T(8,128)(2,1)}, u32[]{:S(2)}) copy-start(bf16[32,2048]{1,0:T(8,128)(2,1)} %param.11) | copy-start | bytes 393220
  265.5 29.5 %all-to-all-start = ((bf16[32,4,4096]{2,0,1:T(8,128)(2,1)}), bf16[32,4,4096]{2,0,1:T(8,128)(2,1)S(1)}, u32[]{:S(2)}, u32[]{:S(2)}) async-start(bf16[32,4,4096]{2,0,1:T(8,128)(2,1)} %bitcast.54), calls=%async_computation | async-start | bytes 2097152 | tf_op jit(solution)/shard_map/all_to_all | solution.py:82
Sparse Core Ops, SparseCore 0:
  44.7 24.4 all-gather.1
  121.7 127.6 all-reduce.2
  264.5 40.2 reduce-scatter.1
where the time goes:
time: 313 us
  waiting for transfers between devices  188 us (60%)
  blocking collectives  61.2 us (20%)
  matrix products  35.3 us (11%)
  between operations  13.2 us (4%)
  other arithmetic  7.19 us (2%)
  local copies, waits for them, and re-layouts  4.2 us (1%)
  starting transfers between devices  3.6 us (1%)
    psum x1, waiting for transfers between devices, body(): summed = lax.psum(partial_sums, 'batch')  128 us
    all_to_all x1, blocking collectives, body(): lax.all_to_all(normed, 'batch', split_axis=1, concat_axis=0, tiled=True)  30.6 us
    all_to_all x1, waiting for transfers between devices, body(): lax.all_to_all(residual, 'batch', split_axis=1, concat_axis=0, tiled=True)  25.9 us
    all_gather x1, waiting for transfers between devices, body(): full_context = lax.all_gather(context, 'mp', axis=1, tiled=True)  24.6 us
    dot_general x1, matrix products, body(): jnp.dot(normed_all, gate_up, preferred_element_type=jnp.float32)  19.7 us
    all_gather x1, blocking collectives, body(): lax.all_gather(key_cache, 'batch', axis=0, tiled=True)  15.8 us
    dot_general x1, matrix products, body(): jnp.dot(hidden, down_weight, preferred_element_type=jnp.float32)  15 us
    all_gather x1, blocking collectives, body(): lax.all_gather(value_cache, 'batch', axis=0, tiled=True)  14.8 us
  transfers between devices with their start and end apart: 4, of which 4 were waited for; matrix products, arithmetic and copies ran while one was open for 0% of the time, Pallas kernels for 0%

commit v1 on v0

v1 whole, which is shorter than its diff:
```python
import functools

import jax
import jax.numpy as jnp
from jax import lax
from jax.experimental import pallas as pl
from jax.experimental.pallas import tpu as pltpu
from jax.sharding import PartitionSpec as P

HEADS = 128
KV_HEADS = 8
HEAD_DIM = 128
PREFIX = 24
ROWS_DEV = 32
CHUNKS = 13
LAG = 2
GATE_SLOTS = 8
DOWN_SLOTS = 4
BLOCKS = 4
MESH = pl.DeviceIdType.MESH
F32 = jnp.float32
BF16 = jnp.bfloat16


def aligned(start, size, step=128):
    return pl.ds(pl.multiple_of(start, step), size)


def kernel(
    nb, nm,
    hidden_hbm, query_hbm, key_hbm, value_hbm, question, prefix_len, gain_hbm,
    gate_hbm, up_hbm, down_hbm,
    out_ref,
    gate_buf, up_buf, down_buf, query, hidden, keys, values, gain, own, res, normed,
    squares, squares_in, inverse, part, rs_out, rs_in, hid, acc,
    sib_out, sib_in, chip_out, chip_in,
    gate_sem, up_sem, down_sem, local_sem, kv_send, kv_recv, a_send, a_recv,
    b_send, b_recv, s_send, s_recv, sq_send, sq_recv, rs_send, rs_recv, ag_send, ag_recv,
    sib_send, sib_recv, chip_send, chip_recv,
):
    b, m = lax.axis_index("batch"), lax.axis_index("mp")
    core, chip, chips = m % 2, m // 2, nm // 2
    rows, features = res.shape
    columns = own.shape[1]
    ratio = features // columns
    half = rows // 2
    width = hid.shape[2]
    mine = rows // nm
    sibling = chip * 2 + 1 - core
    last = nb - 1

    def remote(src, dst, send, recv, to_b, to_m):
        return pltpu.make_async_remote_copy(
            src_ref=src, dst_ref=dst, send_sem=send, recv_sem=recv,
            device_id=(to_b, to_m), device_id_type=MESH,
        )

    def gate_copy(k):
        slot = k % GATE_SLOTS
        at = aligned(k * width, width)
        return (
            pltpu.make_async_copy(gate_hbm.at[:, at], gate_buf.at[slot], gate_sem.at[slot]),
            pltpu.make_async_copy(up_hbm.at[:, at], up_buf.at[slot], up_sem.at[slot]),
        )

    def down_copy(k):
        slot = k % DOWN_SLOTS
        return pltpu.make_async_copy(
            down_hbm.at[aligned(k * width, width)], down_buf.at[slot], down_sem.at[slot]
        )

    group = m * (columns // HEAD_DIM) // (HEADS // KV_HEADS)
    head_at = aligned(group * HEAD_DIM, HEAD_DIM)
    own_rows = aligned(b * ROWS_DEV, ROWS_DEV, ROWS_DEV)
    local = [
        pltpu.make_async_copy(query_hbm, query, local_sem.at[0]),
        pltpu.make_async_copy(
            hidden_hbm.at[:, aligned(m * columns, columns)], hidden, local_sem.at[1]
        ),
        pltpu.make_async_copy(
            gain_hbm.at[:, aligned(b * features, features)], gain, local_sem.at[2]
        ),
        pltpu.make_async_copy(key_hbm.at[:, head_at], keys.at[own_rows], local_sem.at[3]),
        pltpu.make_async_copy(value_hbm.at[:, head_at], values.at[own_rows], local_sem.at[4]),
    ]
    for copy in local:
        copy.start()

    barrier = pltpu.get_barrier_semaphore()

    def greet(to_b, to_m):
        pl.semaphore_signal(barrier, inc=1, device_id=(to_b, to_m), device_id_type=MESH)

    for i in range(1, nb):
        greet((b + i) % nb, m)
    for i in range(1, chips):
        greet(b, ((chip + i) % chips) * 2 + core)
    greet(b, sibling)
    own_feature = m // ratio == b
    if ratio == 2:
        senders = [(i, b * 2 + core) for i in range(nb)]
        targets = chips
    else:
        senders = [(i, b) for i in range(nb)]
        targets = nm
    for from_b, from_m in senders:
        @pl.when(jnp.logical_not(jnp.logical_and(from_b == b, from_m == m)))
        def _(from_b=from_b, from_m=from_m):
            greet(from_b, from_m)
    pl.semaphore_wait(barrier, (nb - 1) + (chips - 1) + 1 + targets - own_feature.astype(jnp.int32))

    kv = []
    for i in range(1, nb):
        for which, (src, dst) in enumerate(((key_hbm, keys), (value_hbm, values))):
            copy = remote(
                src.at[:, head_at], dst.at[own_rows],
                kv_send.at[which, i], kv_recv.at[which, i], (b + i) % nb, m,
            )
            copy.start()
            kv.append(copy)

    def start_gate(k, carry):
        for copy in gate_copy(k):
            copy.start()
        return carry

    def start_down(k, carry):
        down_copy(k).start()
        return carry

    lax.fori_loop(0, GATE_SLOTS, start_gate, 0)
    lax.fori_loop(0, DOWN_SLOTS, start_down, 0)

    acc[...] = jnp.zeros_like(acc)

    row = lax.broadcasted_iota(jnp.int32, (ROWS_DEV, rows), 0)
    key_index = lax.broadcasted_iota(jnp.int32, (ROWS_DEV, rows), 1)
    owner = jnp.zeros((ROWS_DEV, rows), jnp.int32) + b
    for i in range(ROWS_DEV - PREFIX):
        owner = jnp.where(row == PREFIX + i, question[i], owner)
    length = jnp.zeros((ROWS_DEV, rows), jnp.int32)
    for i in range(nb):
        length = jnp.where(owner == i, prefix_len[i], length)
    limit = jnp.where(row < PREFIX, jnp.minimum(row + 1, length), length)
    key_start = owner * ROWS_DEV
    allowed = ((key_index >= key_start) & (key_index < key_start + limit)) | (
        (key_index == b * ROWS_DEV + row) & (row >= PREFIX)
    )
    for copy in local:
        copy.wait()
    for copy in kv:
        copy.wait_recv()
    heads = columns // HEAD_DIM
    stacked = jnp.concatenate(
        [query[:, h * HEAD_DIM : (h + 1) * HEAD_DIM] for h in range(heads)], axis=0
    )
    scores = lax.dot_general(
        stacked, keys[...], (((1,), (1,)), ((), ())), preferred_element_type=F32
    ) * F32(HEAD_DIM**-0.5)
    scores = jnp.where(allowed[None], scores.reshape(heads, ROWS_DEV, rows), F32(-1e30))
    exponent = jnp.exp(scores - jnp.max(scores, axis=-1, keepdims=True))
    attention = exponent / jnp.sum(exponent, axis=-1, keepdims=True)
    context = jnp.dot(
        attention.reshape(heads * ROWS_DEV, rows).astype(BF16), values[...],
        preferred_element_type=F32,
    ).astype(BF16)
    for h in range(heads):
        at = slice(h * HEAD_DIM, (h + 1) * HEAD_DIM)
        own[:, at] = (
            hidden[:, at].astype(F32)
            + context[h * ROWS_DEV : (h + 1) * ROWS_DEV].astype(F32)
        ).astype(BF16)

    squares[...] = jnp.zeros_like(squares)

    def digest(at, size):
        value = res[:, at].astype(F32)
        square = value * value
        total = squares[...]
        for i in range(size // 128):
            total = total + square[:, i * 128 : (i + 1) * 128]
        squares[...] = total
        normed[:, at] = (value * gain[:, at]).astype(BF16)

    if ratio == 2:
        piece = columns // chips
        a_copies = []
        for p in range(chips):
            at = aligned(core * columns + p * piece, piece)
            here = jnp.logical_and(own_feature, chip == p)
            copy = remote(
                own.at[:, p * piece : (p + 1) * piece], res.at[own_rows, at],
                a_send.at[p], a_recv.at[b], chip, p * 2 + core,
            )
            a_copies.append((copy, here))

            @pl.when(jnp.logical_not(here))
            def _(copy=copy):
                copy.start()

            @pl.when(here)
            def _(p=p, at=at):
                res[own_rows, at] = own[:, p * piece : (p + 1) * piece]

        def region(owner_core, owner_chip):
            return aligned(owner_core * columns + owner_chip * piece, piece)

        my_at = region(core, chip)
        for i in range(nb):
            @pl.when(jnp.logical_not(jnp.logical_and(own_feature, b == i)))
            def _(i=i):
                spot = res.at[pl.ds(i * ROWS_DEV, ROWS_DEV), my_at]
                remote(spot, spot, a_send.at[0], a_recv.at[i], b, sibling).wait_recv()

        b_copies, s_copies = [], []
        for i in range(1, chips):
            copy = remote(
                res.at[:, my_at], res.at[:, my_at], b_send.at[i], b_recv.at[i],
                b, ((chip + i) % chips) * 2 + core,
            )
            copy.start()
            b_copies.append(copy)
        copy = remote(res.at[:, my_at], res.at[:, my_at], s_send.at[0], s_recv.at[0], b, sibling)
        copy.start()
        s_copies.append(copy)
        digest(my_at, piece)
        for i in range(1, chips):
            at = region(core, (chip + chips - i) % chips)
            spot = res.at[:, at]
            remote(spot, spot, b_send.at[i], b_recv.at[i], b, sibling).wait_recv()
            copy = remote(spot, spot, s_send.at[i], s_recv.at[i], b, sibling)
            copy.start()
            s_copies.append(copy)
            digest(at, piece)
        for i in range(chips):
            at = region(1 - core, (chip + chips - i) % chips)
            spot = res.at[:, at]
            remote(spot, spot, s_send.at[i], s_recv.at[i], b, sibling).wait_recv()
            digest(at, piece)
    else:
        a_copies, b_copies, s_copies = [], [], []
        for j in range(nm):
            here = jnp.logical_and(own_feature, m == j)
            copy = remote(own, res.at[own_rows], a_send.at[j], a_recv.at[b], m, j)
            a_copies.append((copy, here))

            @pl.when(jnp.logical_not(here))
            def _(copy=copy):
                copy.start()

            @pl.when(here)
            def _():
                res[own_rows, :] = own[...]

        for i in range(nb):
            @pl.when(jnp.logical_not(jnp.logical_and(own_feature, b == i)))
            def _(i=i):
                spot = res.at[pl.ds(i * ROWS_DEV, ROWS_DEV)]
                remote(spot, spot, a_send.at[0], a_recv.at[i], b, sibling).wait_recv()

        digest(slice(0, features), features)

    ends = ((0, 0), (1, last))
    sq_copies = []
    for way, end in ends:
        copy = remote(
            squares.at[pl.ds(way * half, half)], squares_in.at[b],
            sq_send.at[way], sq_recv.at[b], end, m,
        )
        sq_copies.append((copy, end))

        @pl.when(b != end)
        def _(copy=copy):
            copy.start()

    def finish_squares(way, end):
        total = squares[way * half : (way + 1) * half]
        for i in range(nb):
            if i != end:
                remote(
                    squares_in.at[i], squares_in.at[i], sq_send.at[way], sq_recv.at[i], b, sibling
                ).wait_recv()
                total = total + squares_in[i]
        mean = jnp.sum(total, axis=-1, keepdims=True) / F32(features * nb)
        inverse[...] = jnp.broadcast_to(lax.rsqrt(mean + F32(1e-05)), inverse.shape)

    def rs_copy(way, k):
        to_b = jnp.maximum(b - 1, 0) if way == 0 else jnp.minimum(b + 1, last)
        return remote(
            rs_out.at[way, k], rs_in.at[way, k], rs_send.at[way, k], rs_recv.at[way, k], to_b, m
        )

    def ag_copy(way, k):
        to_b = jnp.minimum(b + 1, last) if way == 0 else jnp.maximum(b - 1, 0)
        spot = hid.at[k, pl.ds(way * half, half)]
        return remote(spot, spot, ag_send.at[way, k], ag_recv.at[way, k], to_b, m)

    def reduce_step(way, k):
        at = slice(way * half, (way + 1) * half)
        start, end = (last, 0) if way == 0 else (0, last)

        @pl.when(b == start)
        def _():
            rs_out[way, k] = part[k, at].astype(BF16)
            rs_copy(way, k).start()

        @pl.when(jnp.logical_and(b != start, b != end))
        def _():
            rs_copy(way, k).wait_recv()
            rs_out[way, k] = (part[k, at] + rs_in[way, k].astype(F32)).astype(BF16)
            rs_copy(way, k).start()

        @pl.when(b == end)
        def _():
            @pl.when(k == 0)
            def _():
                finish_squares(way, end)

            rs_copy(way, k).wait_recv()
            scale = inverse[:, :1]
            gate = (part[k, at, :width] + rs_in[way, k, :, :width].astype(F32)) * scale
            up = (part[k, at, width:] + rs_in[way, k, :, width:].astype(F32)) * scale
            hid[k, at] = (gate / (F32(1) + jnp.exp(-gate)) * up).astype(BF16)
            ag_copy(way, k).start()

    def gather_step(way, k):
        ag_copy(way, k).wait_recv()

        @pl.when(b != (last if way == 0 else 0))
        def _():
            ag_copy(way, k).start()

    def inside(k):
        return jnp.logical_and(k >= 0, k < CHUNKS)

    def step(t, carry):
        @pl.when(t < CHUNKS)
        def _():
            slot = t % GATE_SLOTS
            gate_wait, up_wait = gate_copy(t)
            gate_wait.wait()
            part[t, :, :width] = jnp.dot(
                normed[...], gate_buf[slot], preferred_element_type=F32
            )
            up_wait.wait()
            part[t, :, width:] = jnp.dot(
                normed[...], up_buf[slot], preferred_element_type=F32
            )

            @pl.when(t + GATE_SLOTS < CHUNKS)
            def _():
                start_gate(t + GATE_SLOTS, 0)

        for way in range(2):
            hops = last - b if way == 0 else b
            k = t - hops * LAG

            @pl.when(inside(k))
            def _(way=way, k=k):
                reduce_step(way, k)

        for way in range(2):
            hops = b if way == 0 else last - b
            k = t - (last + hops) * LAG

            @pl.when(jnp.logical_and(inside(k), hops > 0))
            def _(way=way, k=k):
                gather_step(way, k)

        k = t - (last + jnp.maximum(b, last - b)) * LAG

        @pl.when(inside(k))
        def _():
            down_copy(k).wait()
            tile = min(512, features)
            for j in range(features // tile):
                at = slice(j * tile, (j + 1) * tile)
                acc[:, at] += jnp.dot(
                    hid[k], down_buf[k % DOWN_SLOTS, :, at], preferred_element_type=F32
                )

            @pl.when(k + DOWN_SLOTS < CHUNKS)
            def _():
                start_down(k + DOWN_SLOTS, 0)

        return carry

    lax.fori_loop(0, CHUNKS + 2 * last * LAG, step, 0)

    block = features // BLOCKS
    sib_copies, chip_copies = [], []

    def rows_of(p, c):
        return pl.ds(pl.multiple_of((p * 2 + c) * mine, mine), mine)

    for j in range(BLOCKS):
        at = slice(j * block, (j + 1) * block)
        for p in range(chips):
            sib_out[j, p] = acc[rows_of(p, 1 - core), at].astype(BF16)
        copy = remote(sib_out.at[j], sib_in.at[j], sib_send.at[j], sib_recv.at[j], b, sibling)
        copy.start()
        sib_copies.append(copy)
    for j in range(BLOCKS):
        at = slice(j * block, (j + 1) * block)
        sib_copies[j].wait_recv()
        for i in range(1, chips):
            to = (chip + i) % chips
            chip_out[j, i] = (
                acc[rows_of(to, core), at] + sib_in[j, to].astype(F32)
            ).astype(BF16)
            copy = remote(
                chip_out.at[j, i], chip_in.at[j, i], chip_send.at[j, i], chip_recv.at[j, i],
                b, to * 2 + core,
            )
            copy.start()
            chip_copies.append(copy)
    for j in range(BLOCKS):
        at = slice(j * block, (j + 1) * block)
        total = acc[rows_of(chip, core), at] + sib_in[j, chip].astype(F32)
        for i in range(1, chips):
            chip_copies[j * (chips - 1) + i - 1].wait_recv()
            total = total + chip_in[j, i].astype(F32)
        out_ref[:, at] = (res[rows_of(chip, core), at].astype(F32) + total).astype(BF16)

    for copy in kv + b_copies + s_copies + sib_copies + chip_copies:
        copy.wait_send()
    for copy, here in a_copies:
        @pl.when(jnp.logical_not(here))
        def _(copy=copy):
            copy.wait_send()
    for copy, end in sq_copies:
        @pl.when(b != end)
        def _(copy=copy):
            copy.wait_send()

    def drain(k, carry):
        for way in range(2):
            stop = 0 if way == 0 else last

            @pl.when(b != stop)
            def _(way=way):
                rs_copy(way, k).wait_send()

            @pl.when(b != last - stop)
            def _(way=way):
                ag_copy(way, k).wait_send()
        return carry

    lax.fori_loop(0, CHUNKS, drain, 0)


def body(
    nb, nm, hidden_in, queries, key_cache, value_cache, question, prefix_len, norm_gain,
    gate_weight, up_weight, down_weight,
):
    features, units = gate_weight.shape
    columns = queries.shape[1]
    rows = nb * ROWS_DEV
    width, half, chips, mine = units // CHUNKS, rows // 2, nm // 2, rows // nm
    block = features // BLOCKS
    dma = pltpu.SemaphoreType.DMA
    scratch = [
        pltpu.VMEM((GATE_SLOTS, features, width), BF16),
        pltpu.VMEM((GATE_SLOTS, features, width), BF16),
        pltpu.VMEM((DOWN_SLOTS, width, features), BF16),
        pltpu.VMEM((ROWS_DEV, columns), BF16),
        pltpu.VMEM((ROWS_DEV, columns), BF16),
        pltpu.VMEM((rows, HEAD_DIM), BF16),
        pltpu.VMEM((rows, HEAD_DIM), BF16),
        pltpu.VMEM((1, features), F32),
        pltpu.VMEM((ROWS_DEV, columns), BF16),
        pltpu.VMEM((rows, features), BF16),
        pltpu.VMEM((rows, features), BF16),
        pltpu.VMEM((rows, 128), F32),
        pltpu.VMEM((nb, half, 128), F32),
        pltpu.VMEM((half, 128), F32),
        pltpu.VMEM((CHUNKS, rows, 2 * width), F32),
        pltpu.VMEM((2, CHUNKS, half, 2 * width), BF16),
        pltpu.VMEM((2, CHUNKS, half, 2 * width), BF16),
        pltpu.VMEM((CHUNKS, rows, width), BF16),
        pltpu.VMEM((rows, features), F32),
        pltpu.VMEM((BLOCKS, chips, mine, block), BF16),
        pltpu.VMEM((BLOCKS, chips, mine, block), BF16),
        pltpu.VMEM((BLOCKS, chips, mine, block), BF16),
        pltpu.VMEM((BLOCKS, chips, mine, block), BF16),
        dma((GATE_SLOTS,)), dma((GATE_SLOTS,)), dma((DOWN_SLOTS,)), dma((5,)),
        dma((2, nb)), dma((2, nb)), dma((nm,)), dma((nb,)),
        dma((chips,)), dma((chips,)), dma((chips,)), dma((chips,)),
        dma((2,)), dma((nb,)),
        dma((2, CHUNKS)), dma((2, CHUNKS)), dma((2, CHUNKS)), dma((2, CHUNKS)),
        dma((BLOCKS,)), dma((BLOCKS,)), dma((BLOCKS, chips)), dma((BLOCKS, chips)),
    ]
    anywhere = pl.BlockSpec(memory_space=pl.ANY)
    scalars = pl.BlockSpec(memory_space=pltpu.SMEM)
    return pl.pallas_call(
        functools.partial(kernel, nb, nm),
        out_shape=jax.ShapeDtypeStruct((mine, features), BF16),
        in_specs=[anywhere] * 4 + [scalars] * 2 + [anywhere] * 4,
        out_specs=pl.BlockSpec(memory_space=pltpu.VMEM),
        scratch_shapes=scratch,
        compiler_params=pltpu.CompilerParams(
            collective_id=0, has_side_effects=True, vmem_limit_bytes=60 * 2**20
        ),
        cost_estimate=pl.CostEstimate(
            flops=6 * rows * features * units, bytes_accessed=6 * features * units,
            transcendentals=0,
        ),
    )(
        hidden_in, queries, key_cache, value_cache, question, prefix_len,
        norm_gain.reshape(1, -1), gate_weight, up_weight, down_weight,
    )


def solution(mesh):
    return jax.shard_map(
        functools.partial(body, mesh.shape["batch"], mesh.shape["mp"]),
        mesh=mesh,
        in_specs=(
            P("batch", None),
            P("batch", "mp"),
            P("batch", None),
            P("batch", None),
            P("batch"),
            P(),
            P(),
            P("batch", "mp"),
            P("batch", "mp"),
            P("mp", "batch"),
        ),
        out_specs=P("mp", "batch"),
        check_vma=False,
    )
```

time: 313 us -> 85.9 us (0.27)
  waiting for transfers between devices: 188 us -> 0 us
  Pallas kernels: 0 us -> 84.2 us
  blocking collectives: 61.2 us -> 0 us
  matrix products: 35.3 us -> 0 us
  between operations: 13.2 us -> 0.01 us
  other arithmetic: 7.19 us -> 0 us
  starting transfers between devices: 3.6 us -> 0 us
    psum x1 -> x0, waiting for transfers between devices: 128 us -> none  [body(): summed = lax.psum(partial_sums, 'batch')]
    pallas_call x0 -> x1, Pallas kernels: none -> 84.2 us  [body(): pl.pallas_call(functools.partial(kernel, nb, nm), out_shape=jax.ShapeDtyp...]
    dot_general x4 -> x0, matrix products: 35.3 us -> none  [the longest x1 19.7 us: body(): jnp.dot(normed_all, gate_up, preferred_element_type=jnp.float32)]
    all_gather x2 -> x0, blocking collectives: 30.7 us -> none  [the longest x1 15.8 us: body(): lax.all_gather(key_cache, 'batch', axis=0, tiled=True)]
    all_to_all x1 -> x0, blocking collectives: 30.6 us -> none  [body(): lax.all_to_all(normed, 'batch', split_axis=1, concat_axis=0, tiled=True)]
    all_to_all x1 -> x0, waiting for transfers between devices: 25.9 us -> none  [body(): lax.all_to_all(residual, 'batch', split_axis=1, concat_axis=0, tiled=True)]
    all_gather x1 -> x0, waiting for transfers between devices: 24.6 us -> none  [body(): full_context = lax.all_gather(context, 'mp', axis=1, tiled=True)]
    reduce_scatter x1 -> x0, waiting for transfers between devices: 9.88 us -> none  [body(): lax.psum_scatter(jnp.dot(hidden, down_weight, preferred_element_type=jnp....]
  transfers between devices with their start and end apart: 4 -> 0, of which waited for: 4 -> 0; matrix products, arithmetic and copies ran while one was open for 0% -> 0% of each run, Pallas kernels for 0% -> 0%
where the time goes in v1:
time: 85.9 us; the launch traced here: 85.8 us
  Pallas kernels  84.2 us (98%)
  local copies, waits for them, and re-layouts  1.57 us (2%)
    pallas_call x1, Pallas kernels, body(): pl.pallas_call(functools.partial(kernel, nb, nm), out_shape=jax.ShapeDtyp...  84.2 us

profile of v1, /device:TPU:0, one launch (start us, length us, event | category | flops | bytes accessed | tf_op | source)
XLA Modules:
  0.0 85.8 jit_solution(10291022564580403993)
XLA Ops:
  0.0 84.2 %shard_map.100 = bf16[16,4096]{1,0:T(8,128)(2,1)} custom-call(bf16[32,16384]{1,0:T(8,128)(2,1)} %hidden_hbm.1, bf16[32,2048]{1,0:T(8,128)(2,1)} %query_hbm.1, bf16[32,1024]{1,0:T(8,128)(2,1)} %key_hbm.1, bf16[32,1024]{1,0:T(8,128)(2,1)} %value_hbm.1, s32[8]{0:T(128)} %question.1, s32[4]{0:T(128)} %prefix_len.1, f32[1,16384]{1,0:T(1,128)} %bitcast.1, ...), custom_call_target="tpu_custom_call" | custom-call | flops 10468982784 | bytes 81788928 | tf_op jit(solution)/shard_map/pallas_call | solution.py:495
  84.2 1.6 %copy.12 = bf16[16,4096]{1,0:T(8,128)(2,1)} copy(bf16[16,4096]{1,0:T(8,128)(2,1)} %shard_map.100) | data formatting | bytes 262144

commit v2 on v1

--- a/solution.py
+++ b/solution.py
@@ -206,20 +206,22 @@
             return aligned(owner_core * columns + owner_chip * piece, piece)
 
         my_at = region(core, chip)
-        for i in range(nb):
-            @pl.when(jnp.logical_not(jnp.logical_and(own_feature, b == i)))
-            def _(i=i):
-                spot = res.at[pl.ds(i * ROWS_DEV, ROWS_DEV), my_at]
-                remote(spot, spot, a_send.at[0], a_recv.at[i], b, sibling).wait_recv()
-
         b_copies, s_copies = [], []
-        for i in range(1, chips):
-            copy = remote(
-                res.at[:, my_at], res.at[:, my_at], b_send.at[i], b_recv.at[i],
-                b, ((chip + i) % chips) * 2 + core,
-            )
-            copy.start()
-            b_copies.append(copy)
+        for ahead in range(nb):
+            source = (b + ahead) % nb
+            spot = res.at[aligned(source * ROWS_DEV, ROWS_DEV, ROWS_DEV), my_at]
+            arrival = remote(spot, spot, a_send.at[0], a_recv.at[source], b, sibling)
+            if ahead == 0:
+                pl.when(jnp.logical_not(own_feature))(arrival.wait_recv)
+            else:
+                arrival.wait_recv()
+            for i in range(1, chips):
+                copy = remote(
+                    spot, spot, b_send.at[ahead, i], b_recv.at[ahead, i],
+                    b, ((chip + i) % chips) * 2 + core,
+                )
+                copy.start()
+                b_copies.append(copy)
         copy = remote(res.at[:, my_at], res.at[:, my_at], s_send.at[0], s_recv.at[0], b, sibling)
         copy.start()
         s_copies.append(copy)
@@ -227,7 +229,12 @@
         for i in range(1, chips):
             at = region(core, (chip + chips - i) % chips)
             spot = res.at[:, at]
-            remote(spot, spot, b_send.at[i], b_recv.at[i], b, sibling).wait_recv()
+            for ahead in range(nb):
+                source = (b + ahead) % nb
+                part_spot = res.at[aligned(source * ROWS_DEV, ROWS_DEV, ROWS_DEV), at]
+                remote(
+                    part_spot, part_spot, b_send.at[ahead, i], b_recv.at[ahead, i], b, sibling
+                ).wait_recv()
             copy = remote(spot, spot, s_send.at[i], s_recv.at[i], b, sibling)
             copy.start()
             s_copies.append(copy)
@@ -330,6 +337,20 @@
         def _():
             ag_copy(way, k).start()
 
+    block = features // BLOCKS
+
+    def rows_of(p, c):
+        return pl.ds(pl.multiple_of((p * 2 + c) * mine, mine), mine)
+
+    def sib_copy(j):
+        return remote(sib_out.at[j], sib_in.at[j], sib_send.at[j], sib_recv.at[j], b, sibling)
+
+    def send_sibling(j):
+        at = slice(j * block, (j + 1) * block)
+        for p in range(chips):
+            sib_out[j, p] = acc[rows_of(p, 1 - core), at].astype(BF16)
+        sib_copy(j).start()
+
     def inside(k):
         return jnp.logical_and(k >= 0, k < CHUNKS)
 
@@ -378,6 +399,14 @@
                 acc[:, at] += jnp.dot(
                     hid[k], down_buf[k % DOWN_SLOTS, :, at], preferred_element_type=F32
                 )
+                ready = [
+                    i for i in range(BLOCKS) if j * tile < (i + 1) * block <= (j + 1) * tile
+                ]
+                if ready:
+                    @pl.when(k == CHUNKS - 1)
+                    def _(ready=ready):
+                        for i in ready:
+                            send_sibling(i)
 
             @pl.when(k + DOWN_SLOTS < CHUNKS)
             def _():
@@ -387,19 +416,8 @@
 
     lax.fori_loop(0, CHUNKS + 2 * last * LAG, step, 0)
 
-    block = features // BLOCKS
-    sib_copies, chip_copies = [], []
-
-    def rows_of(p, c):
-        return pl.ds(pl.multiple_of((p * 2 + c) * mine, mine), mine)
-
-    for j in range(BLOCKS):
-        at = slice(j * block, (j + 1) * block)
-        for p in range(chips):
-            sib_out[j, p] = acc[rows_of(p, 1 - core), at].astype(BF16)
-        copy = remote(sib_out.at[j], sib_in.at[j], sib_send.at[j], sib_recv.at[j], b, sibling)
-        copy.start()
-        sib_copies.append(copy)
+    sib_copies, chip_copies = [sib_copy(j) for j in range(BLOCKS)], []
+
     for j in range(BLOCKS):
         at = slice(j * block, (j + 1) * block)
         sib_copies[j].wait_recv()
@@ -485,7 +503,7 @@
         pltpu.VMEM((BLOCKS, chips, mine, block), BF16),
         dma((GATE_SLOTS,)), dma((GATE_SLOTS,)), dma((DOWN_SLOTS,)), dma((5,)),
         dma((2, nb)), dma((2, nb)), dma((nm,)), dma((nb,)),
-        dma((chips,)), dma((chips,)), dma((chips,)), dma((chips,)),
+        dma((nb, chips)), dma((nb, chips)), dma((chips,)), dma((chips,)),
         dma((2,)), dma((nb,)),
         dma((2, CHUNKS)), dma((2, CHUNKS)), dma((2, CHUNKS)), dma((2, CHUNKS)),
         dma((BLOCKS,)), dma((BLOCKS,)), dma((BLOCKS, chips)), dma((BLOCKS, chips)),

time: 85.9 us -> 85.6 us (level)
  no operation moved by 1% of the time
where the time goes in v2:
time: 85.6 us; the launch traced here: 85.4 us
  Pallas kernels  83.8 us (98%)
  local copies, waits for them, and re-layouts  1.57 us (2%)
    pallas_call x1, Pallas kernels, body(): pl.pallas_call(functools.partial(kernel, nb, nm), out_shape=jax.ShapeDtyp...  83.8 us

profile of v2, /device:TPU:0, one launch (start us, length us, event | category | flops | bytes accessed | tf_op | source)
XLA Modules:
  0.0 85.4 jit_solution(10908969966253090600)
XLA Ops:
  0.0 83.8 %shard_map.100 = bf16[16,4096]{1,0:T(8,128)(2,1)} custom-call(bf16[32,16384]{1,0:T(8,128)(2,1)} %hidden_hbm.1, bf16[32,2048]{1,0:T(8,128)(2,1)} %query_hbm.1, bf16[32,1024]{1,0:T(8,128)(2,1)} %key_hbm.1, bf16[32,1024]{1,0:T(8,128)(2,1)} %value_hbm.1, s32[8]{0:T(128)} %question.1, s32[4]{0:T(128)} %prefix_len.1, f32[1,16384]{1,0:T(1,128)} %bitcast.1, ...), custom_call_target="tpu_custom_call" | custom-call | flops 10468982784 | bytes 81788928 | tf_op jit(solution)/shard_map/pallas_call | solution.py:513
  83.8 1.6 %copy.12 = bf16[16,4096]{1,0:T(8,128)(2,1)} copy(bf16[16,4096]{1,0:T(8,128)(2,1)} %shard_map.100) | data formatting | bytes 262144
